TPU v7x, 256 devices: a whole 4x4x8 slice. The times are simulated.
256 devices in a mesh: slab: 64 (over z, y, core), tile: 4 (over x).
Axes of the slice: x: 4, y: 4, z: 8, core: 2. Of those that a mesh axis runs over, the one named last changes fastest.
Arguments:
- snapshots: bfloat16 [8192, 128, 256], P(('slab', 'tile')), may hold values from -1210 to 1210
- routes: int32 [8192, 1], P(('slab', 'tile')), may hold values from 0 to 3; in each aligned block of 32 rows (0 to 31, 32 to 63, ...) at most 10 rows name the same one
- sketch_matrix: bfloat16 [256, 128], replicated, may hold values from -0.375 to 0.375
Outputs:
- basis_rows: bfloat16 [10240, 128, 128], P(('slab', 'tile'))
- triangle: float32 [128, 128], replicated
Inputs may be any that keep to these rules, and one draw needn't show every extreme that they name: `routes`: among the 32 blocks of one device no owner value appears more than 10 times; a block with value o goes to tile o of its own slab.
All inputs are finite; a program needn't handle non-finite values.
Results may differ from a plain program's by a relative error of at most 0.0065.
Values may be sent and summed in bfloat16 or wider, within the bound.
A program may use at most 64 MiB of HBM per device.

v0:
```python
import math
import jax
import jax.numpy as jnp
from jax import lax
from jax.sharding import PartitionSpec as P

SEND = 10


def slot_selector(routes, tiles, slots):
    destination = routes[:, 0]
    owners = jnp.arange(tiles, dtype=jnp.int32)
    owner_hit = (destination[None, :] == owners[:, None]).astype(jnp.int32)
    earlier = jnp.cumsum(owner_hit, axis=1) - owner_hit
    slot_ids = jnp.arange(slots, dtype=jnp.int32)
    chosen = owner_hit[:, None, :] * (earlier[:, None, :] == slot_ids[None, :, None]).astype(
        jnp.int32
    )
    return chosen.reshape(tiles * slots, routes.shape[0]).astype(jnp.bfloat16)


def place_blocks(selector, block_data):
    block_count, cell_rows, width = block_data.shape
    flattened = jnp.dot(
        selector,
        block_data.reshape(block_count, cell_rows * width),
        preferred_element_type=jnp.float32,
    )
    return flattened.astype(jnp.bfloat16).reshape(selector.shape[0], cell_rows, width)


def global_factor(partial_gram):
    gram_matrix = lax.psum(partial_gram, ("slab", "tile"))
    return jnp.linalg.cholesky(gram_matrix)


def local(snapshots, routes, sketch_matrix):
    n_tile = lax.axis_size("tile")
    n_slab = lax.axis_size("slab")
    block_count, cell_rows, snap_width = snapshots.shape
    sketch_width = sketch_matrix.shape[1]
    cell_root = math.sqrt(block_count * cell_rows * n_slab * n_tile)
    selector = slot_selector(routes, n_tile, SEND)
    outgoing = place_blocks(selector, snapshots).reshape(n_tile, SEND, cell_rows, snap_width)
    product = jnp.einsum(
        "tjrc,cd->tjrd",
        lax.all_to_all(outgoing, "tile", split_axis=0, concat_axis=0, tiled=True),
        sketch_matrix,
        preferred_element_type=jnp.float32,
    )
    sketch = product.astype(jnp.bfloat16)
    sketch_rows = sketch.reshape(-1, sketch_width)
    partial_gram = lax.dot_general(
        sketch_rows, sketch_rows, (((0,), (0,)), ((), ())), preferred_element_type=jnp.float32
    )
    lower_factor = global_factor(partial_gram)
    identity = jnp.eye(sketch_width, dtype=jnp.float32)
    inverse_factor = jax.scipy.linalg.solve_triangular(lower_factor, identity, lower=True)
    wide_rows = sketch_rows.astype(jnp.float32)
    scaled = (
        jnp.dot(wide_rows, inverse_factor.T, precision=lax.Precision.HIGHEST) * cell_root
    ).astype(jnp.bfloat16)
    basis_rows = scaled.reshape(n_tile * SEND, cell_rows, sketch_width)
    return (basis_rows, lower_factor.T / cell_root)


def solution(mesh):
    return jax.shard_map(
        local,
        mesh=mesh,
        in_specs=(P(("slab", "tile"), None, None), P(("slab", "tile"), None), P()),
        out_specs=(P(("slab", "tile"), None, None), P()),
        check_vma=False,
    )
```

profile of v0, /device:TPU:1, one launch (start us, length us, event | category | flops | bytes accessed | tf_op | source)
XLA Modules:
  0.0 325.9 jit_solution(3418719268438397038)
XLA Ops:
  7.2 0.0 copy-start
  7.2 0.0 all-reduce.2.cloned.1.call-start
  7.2 0.7 fusion.5
  7.9 0.2 reduce_window_sum.11
  8.1 0.7 fusion.6
  8.8 2.8 copy.17
  11.6 0.8 convolution_convert_fusion
  12.4 0.6 copy.18
  13.0 35.5 %all_to_all.5 = bf16[4,10,128,256]{3,2,1,0:T(8,128)(2,1)S(1)} all-to-all(bf16[4,10,128,256]{3,2,1,0:T(8,128)(2,1)S(1)} %bitcast.35), channel_id=1, replica_groups=mesh['slab'=64,'tile'=4] {'tile'}, dimensions={0} | all-to-all | bytes 5242880 | tf_op jit(solution)/shard_map/all_to_all | solution.py:47
  48.6 0.0 copy-done
  48.6 0.8 convolution_convert_fusion.1
  49.4 1.2 convolution_bitcast_fusion
  50.6 0.0 all-reduce.2.cloned.1.call-update
  50.6 240.6 %all-reduce.2.cloned.1.call-done = f32[128,128]{0,1:T(8,128)} async-done(((f32[128,128]{0,1:T(8,128)}), f32[128,128]{0,1:T(8,128)}) %all-reduce.2.cloned.1.call-update) | async-done | bytes 65552 | tf_op jit(solution)/shard_map/psum | solution.py:33
  291.2 0.9 copy.11
  292.1 0.9 fusion.4
  293.0 11.7 %cholesky.17 = f32[128,128]{1,0:T(8,128)S(1)} custom-call(f32[128,128]{1,0:T(8,128)S(1)} %fusion.4), custom_call_target="Cholesky" | custom-call | tf_op jit(solution)/shard_map/jit(cholesky)/cholesky | solution.py:34
  304.7 0.6 compare_reduce_fusion
  305.4 0.7 multiply_bitcast_fusion
  306.0 0.7 copy.12
  306.8 9.8 %custom-call.7 = f32[1,128,128]{1,2,0:T(8,128)S(1)} custom-call(f32[1,128,128]{2,1,0:T(8,128)S(1)} %get-tuple-element.7), custom_call_target="InvertDiagBlocksLowerTriangular" | custom-call | tf_op jit(solution)/shard_map/jit(_solve_triangular)/triangular_solve | solution.py:58
  316.6 0.2 fusion.2
  316.8 2.3 fusion
  (3 shorter events, 0.1 us)
Async XLA Ops:
  7.2 41.4 %copy-start = (bf16[256,128]{1,0:T(8,128)(2,1)S(1)}, bf16[256,128]{1,0:T(8,128)(2,1)}, u32[]{:S(2)}) copy-start(bf16[256,128]{1,0:T(8,128)(2,1)} %param.5) | copy-start | bytes 196612
  7.2 284.0 %all-reduce.2.cloned.1.call-start = ((), (), s32[]{:S(2)}) async-start(), calls=%async_computation.1 | async-start | bytes 131072 | tf_op jit(solution)/shard_map/psum | solution.py:33
Sparse Core Ops, SparseCore 0:
  50.7 240.4 all-reduce.1
where the time goes:
time: 326 us
  waiting for transfers between devices  241 us (74%)
  blocking collectives  35.5 us (11%)
  other arithmetic  25.2 us (8%)
  between operations  14.1 us (4%)
  matrix products  5.37 us (2%)
  local copies, waits for them, and re-layouts  5.09 us (2%)
    psum x1, waiting for transfers between devices, global_factor(): gram_matrix = lax.psum(partial_gram, ('slab', 'tile'))  241 us
    all_to_all x1, blocking collectives, local(): lax.all_to_all(outgoing, 'tile', split_axis=0, concat_axis=0, tiled=True)  35.5 us
    another operation x3, other arithmetic, global_factor(): return jnp.linalg.cholesky(gram_matrix)  12.4 us
    another operation x1, other arithmetic, local(): jax.scipy.linalg.solve_triangular(lower_factor, identity, lower=True)  9.81 us
  transfers between devices with their start and end apart: 1, of which 1 were waited for; matrix products, arithmetic and copies ran while one was open for 0% of the time, Pallas kernels for 0%

commit v1 on v0

--- a/solution.py
+++ b/solution.py
@@ -30,7 +30,7 @@
 
 
 def global_factor(partial_gram):
-    gram_matrix = lax.psum(partial_gram, ("slab", "tile"))
+    gram_matrix = lax.psum(lax.psum(partial_gram, "tile"), "slab")
     return jnp.linalg.cholesky(gram_matrix)
 
 

time: 326 us -> 306 us (0.939)
  waiting for transfers between devices: 241 us -> 221 us
    psum x1 -> x2, waiting for transfers between devices: 241 us -> 221 us  [global_factor(): gram_matrix = lax.psum(lax.psum(partial_gram, 'tile'), 'slab')]
  transfers between devices with their start and end apart: 1 -> 2, of which waited for: 1 -> 2; matrix products, arithmetic and copies ran while one was open for 0% -> 0% of each run, Pallas kernels for 0% -> 0%
where the time goes in v1:
time: 306 us
  waiting for transfers between devices  221 us (72%)
  blocking collectives  35.5 us (12%)
  other arithmetic  25.2 us (8%)
  between operations  14.1 us (5%)
  matrix products  5.37 us (2%)
  local copies, waits for them, and re-layouts  5.09 us (2%)
    psum x2, waiting for transfers between devices, global_factor(): gram_matrix = lax.psum(lax.psum(partial_gram, 'tile'), 'slab')  221 us
    all_to_all x1, blocking collectives, local(): lax.all_to_all(outgoing, 'tile', split_axis=0, concat_axis=0, tiled=True)  35.5 us
    another operation x3, other arithmetic, global_factor(): return jnp.linalg.cholesky(gram_matrix)  12.4 us
    another operation x1, other arithmetic, local(): jax.scipy.linalg.solve_triangular(lower_factor, identity, lower=True)  9.81 us
  transfers between devices with their start and end apart: 2, of which 2 were waited for; matrix products, arithmetic and copies ran while one was open for 0% of the time, Pallas kernels for 0%

profile of v1, /device:TPU:1, one launch (start us, length us, event | category | flops | bytes accessed | tf_op | source)
XLA Modules:
  0.0 306.0 jit_solution(7104271662475295378)
XLA Ops:
  7.2 0.0 copy-start
  7.2 0.0 all-reduce.3.cloned.1.call-start
  7.2 0.7 fusion.5
  7.9 0.2 reduce_window_sum.11
  8.1 0.7 fusion.6
  8.8 2.8 copy.17
  11.6 0.8 convolution_convert_fusion
  12.4 0.6 copy.18
  13.0 35.5 %all_to_all.5 = bf16[4,10,128,256]{3,2,1,0:T(8,128)(2,1)S(1)} all-to-all(bf16[4,10,128,256]{3,2,1,0:T(8,128)(2,1)S(1)} %bitcast.35), channel_id=1, replica_groups=mesh['slab'=64,'tile'=4] {'tile'}, dimensions={0} | all-to-all | bytes 5242880 | tf_op jit(solution)/shard_map/all_to_all | solution.py:47
  48.6 0.0 copy-done
  48.6 0.8 convolution_convert_fusion.1
  49.4 1.2 convolution_bitcast_fusion
  50.6 0.0 all-reduce.3.cloned.1.call-update
  50.6 0.0 all-reduce.5.cloned.1.call-start
  50.7 46.4 %all-reduce.3.cloned.1.call-done = f32[128,128]{0,1:T(8,128)} async-done(((f32[128,128]{0,1:T(8,128)}), f32[128,128]{0,1:T(8,128)}) %all-reduce.3.cloned.1.call-update) | async-done | bytes 65552 | tf_op jit(solution)/shard_map/psum | solution.py:33
  97.1 0.0 all-reduce.5.cloned.1.call-update
  97.1 174.1 %all-reduce.5.cloned.1.call-done = f32[128,128]{0,1:T(8,128)} async-done(((f32[128,128]{0,1:T(8,128)}), f32[128,128]{0,1:T(8,128)}) %all-reduce.5.cloned.1.call-update) | async-done | bytes 65552 | tf_op jit(solution)/shard_map/psum | solution.py:33
  271.2 0.9 copy.11
  272.2 0.9 fusion.4
  273.0 11.7 %cholesky.17 = f32[128,128]{1,0:T(8,128)S(1)} custom-call(f32[128,128]{1,0:T(8,128)S(1)} %fusion.4), custom_call_target="Cholesky" | custom-call | tf_op jit(solution)/shard_map/jit(cholesky)/cholesky | solution.py:34
  284.8 0.6 compare_reduce_fusion
  285.4 0.7 multiply_bitcast_fusion
  286.1 0.7 copy.12
  286.8 9.8 %custom-call.7 = f32[1,128,128]{1,2,0:T(8,128)S(1)} custom-call(f32[1,128,128]{2,1,0:T(8,128)S(1)} %get-tuple-element.7), custom_call_target="InvertDiagBlocksLowerTriangular" | custom-call | tf_op jit(solution)/shard_map/jit(_solve_triangular)/triangular_solve | solution.py:58
  296.6 0.2 fusion.2
  296.9 2.3 fusion
  (3 shorter events, 0.1 us)
Async XLA Ops:
  7.2 41.4 %copy-start = (bf16[256,128]{1,0:T(8,128)(2,1)S(1)}, bf16[256,128]{1,0:T(8,128)(2,1)}, u32[]{:S(2)}) copy-start(bf16[256,128]{1,0:T(8,128)(2,1)} %param.5) | copy-start | bytes 196612
  7.2 89.9 %all-reduce.3.cloned.1.call-start = ((), (), s32[]{:S(2)}) async-start(), calls=%async_computation.1 | async-start | bytes 131072 | tf_op jit(solution)/shard_map/psum | solution.py:33
  50.6 220.6 %all-reduce.5.cloned.1.call-start = ((), (), s32[]{:S(2)}) async-start(), calls=%async_computation.2 | async-start | bytes 131072 | tf_op jit(solution)/shard_map/psum | solution.py:33
Sparse Core Ops, SparseCore 0:
  50.7 46.3 all-reduce.2
  101.0 170.2 all-reduce.4

commit v2 on v0

--- a/solution.py
+++ b/solution.py
@@ -30,7 +30,7 @@
 
 
 def global_factor(partial_gram):
-    gram_matrix = lax.psum(partial_gram, ("slab", "tile"))
+    gram_matrix = jnp.sum(lax.all_gather(partial_gram, ("slab", "tile")), axis=0)
     return jnp.linalg.cholesky(gram_matrix)
 
 

time: 326 us -> 218 us (0.67)
  waiting for transfers between devices: 241 us -> 128 us
  other arithmetic: 25.2 us -> 31 us
    psum x1 -> x0, waiting for transfers between devices: 241 us -> none  [global_factor(): gram_matrix = lax.psum(partial_gram, ('slab', 'tile'))]
    all_gather x0 -> x1, waiting for transfers between devices: none -> 128 us  [global_factor(): lax.all_gather(partial_gram, ('slab', 'tile'))]
    reduce_sum x0 -> x1, other arithmetic: none -> 6.59 us  [global_factor(): jnp.sum(lax.all_gather(partial_gram, ('slab', 'tile')), axis=0)]
where the time goes in v2:
time: 218 us
  waiting for transfers between devices  128 us (59%)
  blocking collectives  35.5 us (16%)
  other arithmetic  31 us (14%)
  between operations  14.1 us (6%)
  matrix products  5.36 us (2%)
  local copies, waits for them, and re-layouts  4.25 us (2%)
    all_gather x1, waiting for transfers between devices, global_factor(): lax.all_gather(partial_gram, ('slab', 'tile'))  128 us
    all_to_all x1, blocking collectives, local(): lax.all_to_all(outgoing, 'tile', split_axis=0, concat_axis=0, tiled=True)  35.5 us
    another operation x3, other arithmetic, global_factor(): return jnp.linalg.cholesky(gram_matrix)  12.4 us
    another operation x1, other arithmetic, local(): jax.scipy.linalg.solve_triangular(lower_factor, identity, lower=True)  9.81 us
    reduce_sum x1, other arithmetic, global_factor(): jnp.sum(lax.all_gather(partial_gram, ('slab', 'tile')), axis=0)  6.59 us
  transfers between devices with their start and end apart: 1, of which 1 were waited for; matrix products, arithmetic and copies ran while one was open for 0% of the time, Pallas kernels for 0%

profile of v2, /device:TPU:1, one launch (start us, length us, event | category | flops | bytes accessed | tf_op | source)
XLA Modules:
  0.0 218.1 jit_solution(12798227292656291407)
XLA Ops:
  7.2 0.0 copy-start
  7.2 0.0 all-gather.3.cloned.1.call-start
  7.2 0.7 fusion.5
  7.9 0.2 reduce_window_sum.11
  8.1 0.7 fusion.6
  8.8 2.8 %copy.17 = bf16[4,8,128,256]{3,1,2,0:T(8,128)(2,1)S(1)} copy(bf16[4,8,128,256]{3,2,1,0:T(8,128)(2,1)} %bitcast.41) | data formatting | bytes 4194304
  11.6 0.8 convolution_convert_fusion
  12.4 0.6 copy.18
  13.0 35.5 %all_to_all.5 = bf16[4,10,128,256]{3,2,1,0:T(8,128)(2,1)S(1)} all-to-all(bf16[4,10,128,256]{3,2,1,0:T(8,128)(2,1)S(1)} %bitcast.39), channel_id=1, replica_groups=mesh['slab'=64,'tile'=4] {'tile'}, dimensions={0} | all-to-all | bytes 5242880 | tf_op jit(solution)/shard_map/all_to_all | solution.py:47
  48.6 0.0 copy-done
  48.6 0.8 convolution_convert_fusion.1
  49.4 1.2 convolution_bitcast_fusion
  50.6 0.0 all-gather.3.cloned.1.call-update
  50.6 127.9 %all-gather.3.cloned.1.call-done = f32[32768,128]{1,0:T(8,128)} async-done(((f32[128,128]{1,0:T(8,128)}), f32[32768,128]{1,0:T(8,128)}) %all-gather.3.cloned.1.call-update) | async-done | bytes 16777232 | tf_op jit(solution)/shard_map/all_gather | solution.py:33
  178.5 6.6 %reduce_sum.9 = f32[128,128]{1,0:T(8,128)S(1)} reduce(f32[256,128,128]{2,1,0:T(8,128)} %bitcast.37, f32[]{:T(128)} %constant.48.clone.1), dimensions={0}, to_apply=%region_1.2 | reduce | flops 4177920 | bytes 16842756 | tf_op jit(solution)/shard_map/reduce_sum | solution.py:33
  185.1 0.1 copy.12
  185.2 11.7 %cholesky.17 = f32[128,128]{1,0:T(8,128)S(1)} custom-call(f32[128,128]{1,0:T(8,128)S(1)} %fusion.4), custom_call_target="Cholesky" | custom-call | tf_op jit(solution)/shard_map/jit(cholesky)/cholesky | solution.py:34
  196.9 0.6 compare_reduce_fusion
  197.6 0.7 multiply_bitcast_fusion
  198.2 0.7 copy.13
  199.0 9.8 %custom-call.7 = f32[1,128,128]{1,2,0:T(8,128)S(1)} custom-call(f32[1,128,128]{2,1,0:T(8,128)S(1)} %get-tuple-element.9), custom_call_target="InvertDiagBlocksLowerTriangular" | custom-call | tf_op jit(solution)/shard_map/jit(_solve_triangular)/triangular_solve | solution.py:58
  208.8 0.2 fusion.2
  209.0 2.3 %fusion = bf16[5120,128]{1,0:T(8,128)(2,1)} fusion(bf16[5120,128]{1,0:T(8,128)(2,1)S(1)} %bitcast.36, f32[128,128]{1,0:T(8,128)S(1)} %fusion.2), kind=kOutput, calls=%fused_computation.2 | convolution fusion | flops 1007943680 | bytes 2686976 | tf_op jit(solution)/shard_map/dot_general | solution.py:61
  (4 shorter events, 0.1 us)
Async XLA Ops:
  7.2 41.4 %copy-start = (bf16[256,128]{1,0:T(8,128)(2,1)S(1)}, bf16[256,128]{1,0:T(8,128)(2,1)}, u32[]{:S(2)}) copy-start(bf16[256,128]{1,0:T(8,128)(2,1)} %param.5) | copy-start | bytes 196612
  7.2 171.3 %all-gather.3.cloned.1.call-start = ((), (), s32[]{:S(2)}) async-start(), calls=%async_computation.1 | async-start | bytes 16842752 | tf_op jit(solution)/shard_map/all_gather | solution.py:33
Sparse Core Ops, SparseCore 0:
  50.7 127.6 all-gather.2
